TPU v7x, 1024 devices: a whole 4x8x16 slice. The times are simulated.
1024 devices in a mesh: gx: 8 (over x, y_lo), gy: 4 (over y_hi), gz: 32 (over z, core).
Axes of the slice: x: 4, y: 8 (y_hi: 4, y_lo: 2; y = y_hi * 2 + y_lo), z: 16, core: 2. Of those that a mesh axis runs over, the one named last changes fastest.
Arguments:
- positions: float32 [3, 8, 8, 64, 128], P(None, 'gx', 'gy', 'gz'), may hold values from 0 to 1
- velocities: float32 [3, 8, 8, 64, 128], P(None, 'gx', 'gy', 'gz'), may hold values from -1.8 to 1.8
- species: int32 [8, 8, 64, 128], P('gx', 'gy', 'gz'), may hold values from 0 to 1
- counts: int32 [8, 8, 64], P('gx', 'gy', 'gz'), may hold values from 32 to 128
Outputs:
- new_positions: float32 [3, 8, 8, 64, 128], P(None, 'gx', 'gy', 'gz')
- new_velocities: float32 [3, 8, 8, 64, 128], P(None, 'gx', 'gy', 'gz')
All inputs are finite; a program needn't handle non-finite values.
Results may differ from a plain program's by a relative error of at most 0.0003.
Values sent between devices are 32-bit elements; how exact they have to be, the bound alone decides.
A program may use at most 32 MiB of HBM per device.

v0:
```python
import functools
import itertools

import jax
import jax.numpy as jnp
from jax import lax
from jax.experimental import pallas as pl
from jax.experimental.pallas import tpu as pltpu
from jax.sharding import PartitionSpec as P

MESH = pl.DeviceIdType.MESH
time_step = 0.05
AXES = ("gx", "gy", "gz")
SOURCE = {0: (1, 2), 1: (2, 1), -1: (1, 1)}
TARGET = {0: 1, 1: 0, -1: 3}
DIRECTIONS = sorted(
    (d for d in itertools.product((-1, 0, 1), repeat=3) if d != (0, 0, 0)),
    key=lambda d: -(4 * abs(d[0] * d[1]) + 2 * abs(d[0]) + 2 * abs(d[1]) + abs(d[2])),
)
f32, bf16 = jnp.float32, jnp.bfloat16


def group_of(d):
    return 0 if d[0] == 0 else (1 if d[1] == 0 else 2)


def group_ref(buffer, group):
    return buffer.at[1, pl.ds(0, 3)] if group == 0 else buffer.at[0]


def group_cell(group, index):
    if group == 0:
        return 1, index
    if group == 1:
        return 2 * (index // 2), 1 + index % 2
    return 2 * (index // 2), 3 * (index % 2)


def pieces(value):
    high = value.astype(bf16).astype(f32)
    rest = value - high
    middle = rest.astype(bf16).astype(f32)
    return high, middle, rest - middle


def strength_of(amplitude):
    return jnp.where(amplitude > 1.15, 0.4, jnp.where(amplitude > 0.0, 0.3, 0.0)).astype(f32)


def kernel(
    pos_ref, vel_ref, spec_ref, count_ref, out_pos, out_vel,
    ext, slo, part, rows, reach, lhs, own, acc, total, vel,
    pos_send, pos_recv, slo_send, slo_recv,
):
    place = [lax.axis_index(a) for a in AXES]
    sizes = [lax.axis_size(a) for a in AXES]

    def device(d):
        return tuple(lax.rem(m + k + s, k) for m, k, s in zip(place, sizes, d))

    barrier = pltpu.get_barrier_semaphore()
    for d in DIRECTIONS:
        pl.semaphore_signal(barrier, inc=1, device_id=device(d), device_id_type=MESH)

    row4 = lax.broadcasted_iota(jnp.int32, (4, 128), 0)
    slot = lax.broadcasted_iota(jnp.int32, (1, 128), 1)
    cells = [(y, z) for y in range(2) for z in range(2)]
    for y, z in cells:
        c = 2 * y + z
        present = slot < count_ref[y, z]
        species = spec_ref[y, pl.ds(z, 1)]
        amplitude = jnp.where(present, jnp.where(species == 1, 1.3, 1.0), 0.0).astype(f32)
        inverse_mass = jnp.where(species == 1, 1.6, 1.0).astype(f32)
        ext[0, 1, 1 + y, 1 + z] = jnp.concatenate([pos_ref[k, y, pl.ds(z, 1)] for k in range(3)] + [amplitude], axis=0)
        vel[c] = jnp.concatenate([vel_ref[k, y, pl.ds(z, 1)] for k in range(3)] + [inverse_mass], axis=0)

    pl.semaphore_wait(barrier, len(DIRECTIONS))

    def send(buffer, e, send_sem, recv_sem):
        for d in DIRECTIONS:
            dx, dy, dz = d
            (sy, ny), (sz, nz) = SOURCE[dy], SOURCE[dz]
            pltpu.make_async_remote_copy(
                src_ref=buffer.at[e, 1, pl.ds(sy, ny), pl.ds(sz, nz)],
                dst_ref=buffer.at[e, 1 - dx, pl.ds(TARGET[dy], ny), pl.ds(TARGET[dz], nz)],
                send_sem=send_sem.at[e, group_of(d)],
                recv_sem=recv_sem.at[e, group_of(d)],
                device_id=device(d),
                device_id_type=MESH,
            ).start()

    def wait(buffer, e, sem, group):
        ref = group_ref(buffer.at[e], group)
        pltpu.make_async_copy(ref, ref, sem.at[e, group]).wait()

    def shift_of(ix, iy, iz):
        fx, fy = (jnp.asarray(v, jnp.int32).astype(f32) for v in (ix, iy))
        return jnp.where(row4 == 0, fx - 1.5, jnp.where(row4 == 1, fy - 2.0, float(iz - 2)))

    def prepare(e, group):
        def one(index, carry):
            ix, iy = group_cell(group, index)
            line = 4 * ix + iy
            for iz in range(4):
                lanes = pl.ds(128 * iz, 128)
                tile = ext[e, ix, iy, iz]
                place_ = tile + shift_of(ix, iy, iz)
                square = jnp.sum(jnp.where(row4 < 3, place_ * place_, 0.0), axis=0, keepdims=True)
                h, m, l = pieces(jnp.where(row4 < 3, place_, square))
                one_ = jnp.ones_like(h)
                zero = jnp.zeros_like(h)
                part[line, :, lanes] = jnp.concatenate([h, m, h, m, l, h, one_, zero], axis=0).astype(bf16)
                reach[line, :, lanes] = jnp.concatenate(
                    [jnp.where(row4 < 3, h, 1.0), jnp.where(row4 < 3, m, 0.0), jnp.where(row4 < 3, l, 0.0), zero], axis=0
                ).astype(bf16)
                amplitude = tile[3:4]
                rows[line, 0:1, lanes] = amplitude
                rows[line, 1:2, lanes] = 3.0 * amplitude
                rows[line, 2:3, lanes] = 2.0 * strength_of(amplitude)
            return carry

        lax.fori_loop(0, 4, one, 0)

    def strips(group, body):
        count = (3, 4, 2)[group]

        def one(index, carry):
            y, k = index // count, index % count
            if group == 0:
                line = 4 + y + k
            elif group == 1:
                line = 8 * (k // 2) + 1 + k % 2
            else:
                line = 8 * k + 3 * y
            for z in range(2):
                body(2 * y + z, line, pl.ds(128 * z, 384))
            return carry

        lax.fori_loop(0, 2 * count, one, 0)

    def smooth(c, line, lanes):
        t = jnp.dot(lhs[c], part[line, :, lanes], preferred_element_type=f32)
        return jnp.maximum(t, 0.0)

    def density_strip(c, line, lanes):
        s = smooth(c, line, lanes)
        u = s * s * s * rows[line, 0:1, lanes]
        acc[c] += u[:, :128] + u[:, 128:256] + u[:, 256:]

    def force_strip(c, line, lanes):
        s = smooth(c, line, lanes)
        wide = lambda q: jnp.concatenate([own[c, q]] * 3, axis=1)
        pull = wide(0) * rows[line, 1:2, lanes] + wide(1) * rows[line, 3:4, lanes]
        w = s * (s * pull + wide(2) * rows[line, 2:3, lanes])
        high = w.astype(bf16)
        low = (w - high.astype(f32)).astype(bf16)
        across = (((1,), (1,)), ((), ()))
        g = reach[line, :, lanes]
        total[c] += lax.dot_general(high, g, across, preferred_element_type=f32) + lax.dot_general(
            low, g, across, preferred_element_type=f32
        )

    def across_rows(value):
        return jnp.transpose(jnp.broadcast_to(value, (128, 128)))

    def evaluate(e, carry):
        send(ext, e, pos_send, pos_recv)
        for y, z in cells:
            c = 2 * y + z
            place_ = ext[e, 1, 1 + y, 1 + z] + shift_of(1, 1 + y, 1 + z)
            square = jnp.sum(jnp.where(row4 < 3, place_ * place_, 0.0), axis=0, keepdims=True)
            h, m, l = pieces(2.0 * place_)
            th, tm, tl = pieces(1.0 - square)
            last = lambda v, fill: jnp.where(row4 < 3, v, fill)
            ends = jnp.where(row4 == 0, th, jnp.where(row4 == 1, tm, jnp.where(row4 == 2, tl, 0.0)))
            side = jnp.concatenate(
                [last(h, -1.0), last(h, -1.0), last(m, 0.0), last(m, 0.0), last(h, -1.0), last(l, 0.0), ends, jnp.zeros_like(h)],
                axis=0,
            )
            lhs[c] = jnp.transpose(side).astype(bf16)
            acc[c] = jnp.zeros((128, 128), f32)
            total[c] = jnp.zeros((128, 16), f32)
            amplitude = ext[e, 1, 1 + y, 1 + z][3:4]
            own[c, 1] = across_rows(amplitude)
            own[c, 2] = across_rows(strength_of(amplitude))
        for group in range(3):
            wait(ext, e, pos_recv, group)
            prepare(e, group)
            strips(group, density_strip)
        for y, z in cells:
            c = 2 * y + z
            amplitude = ext[e, 1, 1 + y, 1 + z][3:4]
            level = jnp.sum(jnp.transpose(acc[c]), axis=0, keepdims=True) - amplitude + 1.0
            slo[e, 1, 1 + y, 1 + z] = jnp.where(amplitude > 0.0, -0.5, 0.0) / jnp.sqrt(level)
        send(slo, e, slo_send, slo_recv)
        for y, z in cells:
            own[2 * y + z, 0] = across_rows(slo[e, 1, 1 + y, 1 + z])
        for group in range(3):
            wait(slo, e, slo_recv, group)

            def spread(index, carry):
                ix, iy = group_cell(group, index)
                for iz in range(4):
                    rows[4 * ix + iy, 3:4, pl.ds(128 * iz, 128)] = 3.0 * slo[e, ix, iy, iz]
                return carry

            lax.fori_loop(0, 4, spread, 0)
            strips(group, force_strip)
        kick = jnp.where(e == 1, 2.0, 1.0) * (0.5 * time_step)
        for y, z in cells:
            c = 2 * y + z
            tile = ext[e, 1, 1 + y, 1 + z]
            place_ = tile + shift_of(1, 1 + y, 1 + z)
            r = jnp.transpose(total[c])
            r = r[0:4] + r[4:8] + r[8:12]
            force = -2.0 * (r - place_ * r[3:4])
            v = vel[c]
            v = jnp.where(row4 < 3, v + kick * v[3:4] * force, v)
            vel[c] = v
            ext[e + 1, 1, 1 + y, 1 + z] = jnp.where(row4 < 3, tile + time_step * v, tile)
        return carry

    lax.fori_loop(0, 3, evaluate, 0)
    for y, z in cells:
        for k in range(3):
            out_pos[k, y, pl.ds(z, 1)] = ext[2, 1, 1 + y, 1 + z][k : k + 1]
            out_vel[k, y, pl.ds(z, 1)] = vel[2 * y + z][k : k + 1]

    def drain(e, carry):
        for group in range(3):
            wait(ext, e, pos_send, group)
            wait(slo, e, slo_send, group)
        return carry

    lax.fori_loop(0, 3, drain, 0)


def on_device(positions, velocities, species, counts):
    vmem = pl.BlockSpec(memory_space=pltpu.VMEM)
    shape = jax.ShapeDtypeStruct((3, 2, 2, 128), f32)
    new_positions, new_velocities = pl.pallas_call(
        kernel,
        out_shape=(shape, shape),
        in_specs=[vmem, vmem, vmem, pl.BlockSpec(memory_space=pltpu.SMEM)],
        out_specs=(vmem, vmem),
        scratch_shapes=[
            pltpu.VMEM((4, 3, 4, 4, 4, 128), f32),
            pltpu.VMEM((3, 3, 4, 4, 1, 128), f32),
            pltpu.VMEM((12, 32, 512), bf16),
            pltpu.VMEM((12, 8, 512), f32),
            pltpu.VMEM((12, 16, 512), bf16),
            pltpu.VMEM((4, 128, 32), bf16),
            pltpu.VMEM((4, 3, 128, 128), f32),
            pltpu.VMEM((4, 128, 128), f32),
            pltpu.VMEM((4, 128, 16), f32),
            pltpu.VMEM((4, 4, 128), f32),
        ]
        + [pltpu.SemaphoreType.DMA((3, 3))] * 4,
        compiler_params=pltpu.CompilerParams(
            collective_id=0, has_side_effects=True, vmem_limit_bytes=32 * 1024 * 1024
        ),
    )(positions[:, 0], velocities[:, 0], species[0], counts[0])
    return new_positions[:, None], new_velocities[:, None]


def solution(mesh):
    return jax.shard_map(
        on_device,
        mesh=mesh,
        in_specs=(
            P(None, "gx", "gy", "gz", None),
            P(None, "gx", "gy", "gz", None),
            P("gx", "gy", "gz", None),
            P("gx", "gy", "gz"),
        ),
        out_specs=(P(None, "gx", "gy", "gz", None), P(None, "gx", "gy", "gz", None)),
        check_vma=False,
    )
```

profile of v0, /device:TPU:1, one launch (start us, length us, event | category | flops | bytes accessed | tf_op | source)
XLA Modules:
  0.0 96.3 jit_solution(5208281483496796460)
XLA Ops:
  0.6 0.0 copy-start
  0.6 0.0 copy-start.3
  0.7 0.7 copy-done
  1.3 0.0 copy-done.3
  1.3 0.0 copy-start.1
  1.3 0.7 copy-done.1
  2.0 0.0 copy-start.2
  2.0 0.7 copy-done.2
  2.7 92.4 %shard_map.59 = (f32[3,2,2,128]{3,2,1,0:T(2,128)S(1)}, f32[3,2,2,128]{3,2,1,0:T(2,128)S(1)}) custom-call(f32[3,2,2,128]{3,2,1,0:T(2,128)S(1)} %bitcast.12, f32[3,2,2,128]{3,2,1,0:T(2,128)S(1)} %bitcast.13, s32[2,2,128]{2,1,0:T(2,128)S(1)} %bitcast.14, s32[2,2]{1,0:T(2,128)S(1)} %bitcast.15), custom_call_target="tpu_custom_call" | custom-call | tf_op jit(solution)/shard_map/pallas_call | solution.py:241
  95.1 0.6 copy.10
  95.7 0.6 copy.11
Async XLA Ops:
  0.6 0.7 copy-start
  0.6 0.7 copy-start.3
  1.3 0.7 copy-start.1
  2.0 0.7 copy-start.2
where the time goes:
time: 96.6 us; the launch traced here: 96.3 us
  Pallas kernels  92.4 us (96%)
  local copies, waits for them, and re-layouts  3.24 us (3%)
    pallas_call x1, Pallas kernels, on_device(): pl.pallas_call(kernel, out_shape=(shape, shape), in_specs=[vmem, vmem, vm...  92.4 us
    unnamed x10, local copies, waits for them, and re-layouts  3.24 us

commit v1 on v0

--- a/solution.py
+++ b/solution.py
@@ -18,6 +18,7 @@
     key=lambda d: -(4 * abs(d[0] * d[1]) + 2 * abs(d[0]) + 2 * abs(d[1]) + abs(d[2])),
 )
 f32, bf16 = jnp.float32, jnp.bfloat16
+CHUNKS = (128, 64, 128)
 
 
 def group_of(d):
@@ -49,7 +50,7 @@
 
 def kernel(
     pos_ref, vel_ref, spec_ref, count_ref, out_pos, out_vel,
-    ext, slo, part, rows, reach, lhs, own, acc, total, vel,
+    ext, slo, part, rows, lhs, own, near, acc, total, vel,
     pos_send, pos_recv, slo_send, slo_recv,
 ):
     place = [lax.axis_index(a) for a in AXES]
@@ -96,6 +97,9 @@
     def shift_of(ix, iy, iz):
         fx, fy = (jnp.asarray(v, jnp.int32).astype(f32) for v in (ix, iy))
         return jnp.where(row4 == 0, fx - 1.5, jnp.where(row4 == 1, fy - 2.0, float(iz - 2)))
+
+    def keep(line, k, lanes, value):
+        rows[line, k, :, lanes] = jnp.broadcast_to(value, (8, 128))
 
     def prepare(e, group):
         def one(index, carry):
@@ -110,55 +114,98 @@
                 one_ = jnp.ones_like(h)
                 zero = jnp.zeros_like(h)
                 part[line, :, lanes] = jnp.concatenate([h, m, h, m, l, h, one_, zero], axis=0).astype(bf16)
-                reach[line, :, lanes] = jnp.concatenate(
-                    [jnp.where(row4 < 3, h, 1.0), jnp.where(row4 < 3, m, 0.0), jnp.where(row4 < 3, l, 0.0), zero], axis=0
-                ).astype(bf16)
                 amplitude = tile[3:4]
-                rows[line, 0:1, lanes] = amplitude
-                rows[line, 1:2, lanes] = 3.0 * amplitude
-                rows[line, 2:3, lanes] = 2.0 * strength_of(amplitude)
+                keep(line, 0, lanes, amplitude)
+                keep(line, 1, lanes, 2.0 * strength_of(amplitude))
+                for k in range(3):
+                    keep(line, 2 + k, lanes, place_[k : k + 1])
             return carry
 
         lax.fori_loop(0, 4, one, 0)
 
-    def strips(group, body):
-        count = (3, 4, 2)[group]
-
+    def lines_of(group, y):
+        if group == 0:
+            return [4 + y + k for k in range(3)]
+        if group == 1:
+            return [1, 2, 9, 10]
+        return [3 * y, 8 + 3 * y]
+
+    def smooth(group):
+        def one(c, line, z):
+            t = jnp.dot(lhs[c], part[line, :, pl.ds(128 * z, 384)], preferred_element_type=f32)
+            near[c, line] = jnp.maximum(t, 0.0)
+
+        if group == 2:
+            for y, z in cells:
+                for line in lines_of(2, y):
+                    one(2 * y + z, line, z)
+        else:
+
+            def step(k, carry):
+                for y, z in cells:
+                    one(2 * y + z, 4 + y + k if group == 0 else 8 * (k // 2) + 1 + k % 2, z)
+                return carry
+
+            lax.fori_loop(0, 3 + group, step, 0)
+
+    def sweep(count, body):
         def one(index, carry):
-            y, k = index // count, index % count
-            if group == 0:
-                line = 4 + y + k
-            elif group == 1:
-                line = 8 * (k // 2) + 1 + k % 2
-            else:
-                line = 8 * k + 3 * y
-            for z in range(2):
-                body(2 * y + z, line, pl.ds(128 * z, 384))
+            parts = 128 // count
+            c = index // parts
+            body(c, c // 2, c % 2, pl.ds(pl.multiple_of(count * (index % parts), count), count))
             return carry
 
-        lax.fori_loop(0, 2 * count, one, 0)
-
-    def smooth(c, line, lanes):
-        t = jnp.dot(lhs[c], part[line, :, lanes], preferred_element_type=f32)
-        return jnp.maximum(t, 0.0)
-
-    def density_strip(c, line, lanes):
-        s = smooth(c, line, lanes)
-        u = s * s * s * rows[line, 0:1, lanes]
-        acc[c] += u[:, :128] + u[:, 128:256] + u[:, 256:]
-
-    def force_strip(c, line, lanes):
-        s = smooth(c, line, lanes)
-        wide = lambda q: jnp.concatenate([own[c, q]] * 3, axis=1)
-        pull = wide(0) * rows[line, 1:2, lanes] + wide(1) * rows[line, 3:4, lanes]
-        w = s * (s * pull + wide(2) * rows[line, 2:3, lanes])
-        high = w.astype(bf16)
-        low = (w - high.astype(f32)).astype(bf16)
-        across = (((1,), (1,)), ((), ()))
-        g = reach[line, :, lanes]
-        total[c] += lax.dot_general(high, g, across, preferred_element_type=f32) + lax.dot_general(
-            low, g, across, preferred_element_type=f32
-        )
+        lax.fori_loop(0, 4 * (128 // count), one, 0)
+
+    def tiles(lines, z):
+        for line in lines:
+            for k in range(3):
+                yield line, pl.ds(128 * k, 128), pl.ds(pl.multiple_of(128 * (z + k), 128), 128)
+
+    def fold(value):
+        return value.reshape(-1, 8, 128)
+
+    def add_density(group):
+        def body(c, y, z, chunk):
+            level = fold(acc[c, 0, chunk])
+            for line, at, lanes in tiles(lines_of(group, y), z):
+                s = fold(near[c, line, chunk, at])
+                level = level + s * s * (s * rows[line, 0, :, lanes])
+            acc[c, 0, chunk] = level.reshape(-1, 128)
+
+        sweep(CHUNKS[0], body)
+
+    def first_forces():
+        def body(c, y, z, chunk):
+            slope, strength = fold(own[c, 0, chunk]), fold(own[c, 1, chunk])
+            sums = [jnp.zeros(slope.shape, f32) for _ in range(4)]
+            for line, at, lanes in tiles([4 * ix + y + k for ix in range(3) for k in range(3)], z):
+                s = fold(near[c, line, chunk, at])
+                square = s * s
+                near[c, line, chunk, at] = square.reshape(-1, 128)
+                w = square * (slope * rows[line, 0, :, lanes]) + s * (strength * rows[line, 1, :, lanes])
+                sums[3] = sums[3] + w
+                for k in range(3):
+                    sums[k] = sums[k] + w * rows[line, 2 + k, :, lanes]
+            for k in range(4):
+                acc[c, k, chunk] = sums[k].reshape(-1, 128)
+
+        sweep(CHUNKS[1], body)
+
+    def add_forces(group):
+        def body(c, y, z, chunk):
+            sums = [fold(acc[c, k, chunk]) for k in range(4)]
+            for line, at, lanes in tiles(lines_of(group, y), z):
+                square = fold(near[c, line, chunk, at])
+                for k in range(4):
+                    sums[k] = sums[k] + square * rows[line, 5 + k, :, lanes]
+            for k in range(4):
+                acc[c, k, chunk] = sums[k].reshape(-1, 128)
+
+        sweep(CHUNKS[2], body)
+
+    def lane_sums(c):
+        return jnp.concatenate([jnp.sum(jnp.transpose(acc[c, k]), axis=0, keepdims=True) for k in range(4)], axis=0)
 
     def across_rows(value):
         return jnp.transpose(jnp.broadcast_to(value, (128, 128)))
@@ -178,41 +225,47 @@
                 axis=0,
             )
             lhs[c] = jnp.transpose(side).astype(bf16)
-            acc[c] = jnp.zeros((128, 128), f32)
-            total[c] = jnp.zeros((128, 16), f32)
-            amplitude = ext[e, 1, 1 + y, 1 + z][3:4]
-            own[c, 1] = across_rows(amplitude)
-            own[c, 2] = across_rows(strength_of(amplitude))
+            acc[c, 0] = jnp.zeros((128, 128), f32)
+            own[c, 1] = across_rows(strength_of(ext[e, 1, 1 + y, 1 + z][3:4]))
         for group in range(3):
             wait(ext, e, pos_recv, group)
             prepare(e, group)
-            strips(group, density_strip)
+            smooth(group)
+            add_density(group)
         for y, z in cells:
             c = 2 * y + z
             amplitude = ext[e, 1, 1 + y, 1 + z][3:4]
-            level = jnp.sum(jnp.transpose(acc[c]), axis=0, keepdims=True) - amplitude + 1.0
+            level = jnp.sum(jnp.transpose(acc[c, 0]), axis=0, keepdims=True) - amplitude + 1.0
             slo[e, 1, 1 + y, 1 + z] = jnp.where(amplitude > 0.0, -0.5, 0.0) / jnp.sqrt(level)
         send(slo, e, slo_send, slo_recv)
         for y, z in cells:
-            own[2 * y + z, 0] = across_rows(slo[e, 1, 1 + y, 1 + z])
+            own[2 * y + z, 0] = across_rows(3.0 * slo[e, 1, 1 + y, 1 + z])
+        first_forces()
+        for c in range(4):
+            total[c] = lane_sums(c)
+            for k in range(4):
+                acc[c, k] = jnp.zeros((128, 128), f32)
         for group in range(3):
             wait(slo, e, slo_recv, group)
 
             def spread(index, carry):
                 ix, iy = group_cell(group, index)
                 for iz in range(4):
-                    rows[4 * ix + iy, 3:4, pl.ds(128 * iz, 128)] = 3.0 * slo[e, ix, iy, iz]
+                    line, lanes = 4 * ix + iy, pl.ds(128 * iz, 128)
+                    slope = 3.0 * slo[e, ix, iy, iz]
+                    keep(line, 8, lanes, slope)
+                    for k in range(3):
+                        rows[line, 5 + k, :, lanes] = slope * rows[line, 2 + k, :, lanes]
                 return carry
 
             lax.fori_loop(0, 4, spread, 0)
-            strips(group, force_strip)
+            add_forces(group)
         kick = jnp.where(e == 1, 2.0, 1.0) * (0.5 * time_step)
         for y, z in cells:
             c = 2 * y + z
             tile = ext[e, 1, 1 + y, 1 + z]
             place_ = tile + shift_of(1, 1 + y, 1 + z)
-            r = jnp.transpose(total[c])
-            r = r[0:4] + r[4:8] + r[8:12]
+            r = total[c] + tile[3:4] * lane_sums(c)
             force = -2.0 * (r - place_ * r[3:4])
             v = vel[c]
             v = jnp.where(row4 < 3, v + kick * v[3:4] * force, v)
@@ -247,12 +300,12 @@
             pltpu.VMEM((4, 3, 4, 4, 4, 128), f32),
             pltpu.VMEM((3, 3, 4, 4, 1, 128), f32),
             pltpu.VMEM((12, 32, 512), bf16),
-            pltpu.VMEM((12, 8, 512), f32),
-            pltpu.VMEM((12, 16, 512), bf16),
+            pltpu.VMEM((12, 9, 8, 512), f32),
             pltpu.VMEM((4, 128, 32), bf16),
-            pltpu.VMEM((4, 3, 128, 128), f32),
-            pltpu.VMEM((4, 128, 128), f32),
-            pltpu.VMEM((4, 128, 16), f32),
+            pltpu.VMEM((4, 2, 128, 128), f32),
+            pltpu.VMEM((4, 12, 128, 384), f32),
+            pltpu.VMEM((4, 4, 128, 128), f32),
+            pltpu.VMEM((4, 4, 128), f32),
             pltpu.VMEM((4, 4, 128), f32),
         ]
         + [pltpu.SemaphoreType.DMA((3, 3))] * 4,

time: 96.6 us -> 73 us (0.76)
  Pallas kernels: 92.4 us -> 68.9 us
    pallas_call x1, Pallas kernels: 92.4 us -> 68.9 us  [on_device(): pl.pallas_call(kernel, out_shape=(shape, shape), in_specs=[vmem, vmem, vm...]
where the time goes in v1:
time: 73 us; the launch traced here: 72.8 us
  Pallas kernels  68.9 us (94%)
  local copies, waits for them, and re-layouts  3.24 us (4%)
    pallas_call x1, Pallas kernels, on_device(): pl.pallas_call(kernel, out_shape=(shape, shape), in_specs=[vmem, vmem, vm...  68.9 us
    unnamed x10, local copies, waits for them, and re-layouts  3.24 us

profile of v1, /device:TPU:1, one launch (start us, length us, event | category | flops | bytes accessed | tf_op | source)
XLA Modules:
  0.0 72.8 jit_solution(7488747601559490697)
XLA Ops:
  0.6 0.0 copy-start
  0.6 0.0 copy-start.3
  0.7 0.7 copy-done
  1.3 0.0 copy-done.3
  1.3 0.0 copy-start.1
  1.3 0.7 copy-done.1
  2.0 0.0 copy-start.2
  2.0 0.7 copy-done.2
  2.7 68.9 %shard_map.59 = (f32[3,2,2,128]{3,2,1,0:T(2,128)S(1)}, f32[3,2,2,128]{3,2,1,0:T(2,128)S(1)}) custom-call(f32[3,2,2,128]{3,2,1,0:T(2,128)S(1)} %bitcast.12, f32[3,2,2,128]{3,2,1,0:T(2,128)S(1)} %bitcast.13, s32[2,2,128]{2,1,0:T(2,128)S(1)} %bitcast.14, s32[2,2]{1,0:T(2,128)S(1)} %bitcast.15), custom_call_target="tpu_custom_call" | custom-call | tf_op jit(solution)/shard_map/pallas_call | solution.py:294
  71.6 0.6 copy.10
  72.2 0.6 copy.11
Async XLA Ops:
  0.6 0.7 copy-start
  0.6 0.7 copy-start.3
  1.3 0.7 copy-start.1
  2.0 0.7 copy-start.2

commit v2 on v1

--- a/solution.py
+++ b/solution.py
@@ -18,23 +18,19 @@
     key=lambda d: -(4 * abs(d[0] * d[1]) + 2 * abs(d[0]) + 2 * abs(d[1]) + abs(d[2])),
 )
 f32, bf16 = jnp.float32, jnp.bfloat16
-CHUNKS = (128, 64, 128)
+CHUNK = 64
 
 
 def group_of(d):
-    return 0 if d[0] == 0 else (1 if d[1] == 0 else 2)
+    if d[0] == 0:
+        return 0 if d[1] == 0 else 1
+    return {0: 2, 1: 3, -1: 4}[d[1]]
 
 
 def group_ref(buffer, group):
-    return buffer.at[1, pl.ds(0, 3)] if group == 0 else buffer.at[0]
-
-
-def group_cell(group, index):
-    if group == 0:
-        return 1, index
-    if group == 1:
-        return 2 * (index // 2), 1 + index % 2
-    return 2 * (index // 2), 3 * (index % 2)
+    if isinstance(group, int) and group < 3:
+        return (buffer.at[1, 0], buffer.at[1, pl.ds(0, 2)], buffer.at[0])[group]
+    return buffer.at[1, pl.ds(0, 2)]
 
 
 def pieces(value):
@@ -49,9 +45,9 @@
 
 
 def kernel(
-    pos_ref, vel_ref, spec_ref, count_ref, out_pos, out_vel,
+    pos_hbm, vel_hbm, spec_hbm, count_hbm, out_pos, out_vel,
     ext, slo, part, rows, lhs, own, near, acc, total, vel,
-    pos_send, pos_recv, slo_send, slo_recv,
+    pos_ref, vel_ref, spec_ref, count_ref, pos_send, pos_recv, slo_send, slo_recv, load_sem,
 ):
     place = [lax.axis_index(a) for a in AXES]
     sizes = [lax.axis_size(a) for a in AXES]
@@ -62,13 +58,24 @@
     barrier = pltpu.get_barrier_semaphore()
     for d in DIRECTIONS:
         pl.semaphore_signal(barrier, inc=1, device_id=device(d), device_id_type=MESH)
+
+    loads = [
+        pltpu.make_async_copy(source, target, load_sem.at[k])
+        for k, (source, target) in enumerate(
+            [(pos_hbm, pos_ref), (spec_hbm, spec_ref), (count_hbm, count_ref), (vel_hbm, vel_ref)]
+        )
+    ]
+    for load in loads:
+        load.start()
+    for load in loads:
+        load.wait()
 
     row4 = lax.broadcasted_iota(jnp.int32, (4, 128), 0)
     slot = lax.broadcasted_iota(jnp.int32, (1, 128), 1)
     cells = [(y, z) for y in range(2) for z in range(2)]
     for y, z in cells:
         c = 2 * y + z
-        present = slot < count_ref[y, z]
+        present = slot < count_ref[pl.ds(y, 1), pl.ds(z, 1)]
         species = spec_ref[y, pl.ds(z, 1)]
         amplitude = jnp.where(present, jnp.where(species == 1, 1.3, 1.0), 0.0).astype(f32)
         inverse_mass = jnp.where(species == 1, 1.6, 1.0).astype(f32)
@@ -101,10 +108,10 @@
     def keep(line, k, lanes, value):
         rows[line, k, :, lanes] = jnp.broadcast_to(value, (8, 128))
 
-    def prepare(e, group):
+    def prepare(e, count, line_at):
         def one(index, carry):
-            ix, iy = group_cell(group, index)
-            line = 4 * ix + iy
+            line = line_at(index)
+            ix, iy = line // 4, line % 4
             for iz in range(4):
                 lanes = pl.ds(128 * iz, 128)
                 tile = ext[e, ix, iy, iz]
@@ -121,32 +128,59 @@
                     keep(line, 2 + k, lanes, place_[k : k + 1])
             return carry
 
-        lax.fori_loop(0, 4, one, 0)
-
-    def lines_of(group, y):
+        lax.fori_loop(0, count, one, 0)
+
+    last = lax.rem(place[0] + 1, 2)
+    side_of = {3: 1 - last, 4: last}
+
+    fetched = {
+        0: (2, lambda k: 5 + k),
+        1: (2, lambda k: 4 + 3 * k),
+        2: (4, lambda k: 8 * (k // 2) + 1 + k % 2),
+        3: (2, lambda k: 8 * k + 3 * side_of[3]),
+        4: (2, lambda k: 8 * k + 3 * side_of[4]),
+    }
+
+    def met(group):
         if group == 0:
-            return [4 + y + k for k in range(3)]
+            return [(y, [5, 6]) for y in range(2)]
         if group == 1:
-            return [1, 2, 9, 10]
-        return [3 * y, 8 + 3 * y]
-
-    def smooth(group):
-        def one(c, line, z):
-            t = jnp.dot(lhs[c], part[line, :, pl.ds(128 * z, 384)], preferred_element_type=f32)
-            near[c, line] = jnp.maximum(t, 0.0)
-
+            return [(y, [4 + 3 * y]) for y in range(2)]
         if group == 2:
-            for y, z in cells:
-                for line in lines_of(2, y):
-                    one(2 * y + z, line, z)
+            return [(y, [1, 2, 9, 10]) for y in range(2)]
+        y = side_of[group]
+        return [(y, [3 * y, 8 + 3 * y])]
+
+    def strip(c, line, z):
+        t = jnp.dot(lhs[c], part[line, :, pl.ds(128 * z, 384)], preferred_element_type=f32)
+        s = jnp.maximum(t, 0.0)
+        near[c, line] = s
+        return s
+
+    def weighted(s, line, z):
+        out = None
+        for k in range(3):
+            v = fold(s[:, 128 * k : 128 * k + 128])
+            v = v * v * (v * rows[line, 0, :, pl.ds(128 * (z + k), 128)])
+            out = v if out is None else out + v
+        return out.reshape(128, 128)
+
+    def densities(group):
+        if group == 2:
+
+            def step(k, carry):
+                line = 8 * (k // 2) + 1 + k % 2
+                for y, z in cells:
+                    c = 2 * y + z
+                    acc[c, 0] += weighted(strip(c, line, z), line, z)
+                return carry
+
+            lax.fori_loop(0, 4, step, 0)
         else:
-
-            def step(k, carry):
-                for y, z in cells:
-                    one(2 * y + z, 4 + y + k if group == 0 else 8 * (k // 2) + 1 + k % 2, z)
-                return carry
-
-            lax.fori_loop(0, 3 + group, step, 0)
+            for y, lines in met(group):
+                for z in range(2):
+                    c = 2 * y + z
+                    acc[c, 0] += sum(weighted(strip(c, line, z), line, z) for line in lines)
 
     def sweep(count, body):
         def one(index, carry):
@@ -164,16 +198,6 @@
 
     def fold(value):
         return value.reshape(-1, 8, 128)
-
-    def add_density(group):
-        def body(c, y, z, chunk):
-            level = fold(acc[c, 0, chunk])
-            for line, at, lanes in tiles(lines_of(group, y), z):
-                s = fold(near[c, line, chunk, at])
-                level = level + s * s * (s * rows[line, 0, :, lanes])
-            acc[c, 0, chunk] = level.reshape(-1, 128)
-
-        sweep(CHUNKS[0], body)
 
     def first_forces():
         def body(c, y, z, chunk):
@@ -190,25 +214,38 @@
             for k in range(4):
                 acc[c, k, chunk] = sums[k].reshape(-1, 128)
 
-        sweep(CHUNKS[1], body)
+        sweep(CHUNK, body)
 
     def add_forces(group):
-        def body(c, y, z, chunk):
-            sums = [fold(acc[c, k, chunk]) for k in range(4)]
-            for line, at, lanes in tiles(lines_of(group, y), z):
-                square = fold(near[c, line, chunk, at])
+        def body(c, lines, z):
+            sums = [fold(acc[c, k]) for k in range(4)]
+            for line, at, lanes in tiles(lines, z):
+                square = fold(near[c, line, :, at])
                 for k in range(4):
                     sums[k] = sums[k] + square * rows[line, 5 + k, :, lanes]
             for k in range(4):
-                acc[c, k, chunk] = sums[k].reshape(-1, 128)
-
-        sweep(CHUNKS[2], body)
+                acc[c, k] = sums[k].reshape(128, 128)
+
+        def one(c, carry):
+            y, z = c // 2, c % 2
+            body(c, {0: [5, 6], 1: [4 + 3 * y], 2: [1, 2, 9, 10]}[group], z)
+            return carry
+
+        if group < 3:
+            lax.fori_loop(0, 4, one, 0)
+        else:
+            y = side_of[group]
+            for z in range(2):
+                body(2 * y + z, [3 * y, 8 + 3 * y], z)
 
     def lane_sums(c):
         return jnp.concatenate([jnp.sum(jnp.transpose(acc[c, k]), axis=0, keepdims=True) for k in range(4)], axis=0)
 
     def across_rows(value):
         return jnp.transpose(jnp.broadcast_to(value, (128, 128)))
+
+    def arrival(group):
+        return group if group < 3 else 3 + side_of[group]
 
     def evaluate(e, carry):
         send(ext, e, pos_send, pos_recv)
@@ -218,20 +255,19 @@
             square = jnp.sum(jnp.where(row4 < 3, place_ * place_, 0.0), axis=0, keepdims=True)
             h, m, l = pieces(2.0 * place_)
             th, tm, tl = pieces(1.0 - square)
-            last = lambda v, fill: jnp.where(row4 < 3, v, fill)
+            end = lambda v, fill: jnp.where(row4 < 3, v, fill)
             ends = jnp.where(row4 == 0, th, jnp.where(row4 == 1, tm, jnp.where(row4 == 2, tl, 0.0)))
             side = jnp.concatenate(
-                [last(h, -1.0), last(h, -1.0), last(m, 0.0), last(m, 0.0), last(h, -1.0), last(l, 0.0), ends, jnp.zeros_like(h)],
+                [end(h, -1.0), end(h, -1.0), end(m, 0.0), end(m, 0.0), end(h, -1.0), end(l, 0.0), ends, jnp.zeros_like(h)],
                 axis=0,
             )
             lhs[c] = jnp.transpose(side).astype(bf16)
             acc[c, 0] = jnp.zeros((128, 128), f32)
             own[c, 1] = across_rows(strength_of(ext[e, 1, 1 + y, 1 + z][3:4]))
-        for group in range(3):
-            wait(ext, e, pos_recv, group)
-            prepare(e, group)
-            smooth(group)
-            add_density(group)
+        for group in range(5):
+            wait(ext, e, pos_recv, arrival(group))
+            prepare(e, *fetched[group])
+            densities(group)
         for y, z in cells:
             c = 2 * y + z
             amplitude = ext[e, 1, 1 + y, 1 + z][3:4]
@@ -245,20 +281,22 @@
             total[c] = lane_sums(c)
             for k in range(4):
                 acc[c, k] = jnp.zeros((128, 128), f32)
-        for group in range(3):
-            wait(slo, e, slo_recv, group)
+        for group in range(5):
+            wait(slo, e, slo_recv, arrival(group))
+            count, line_at = fetched[group]
 
             def spread(index, carry):
-                ix, iy = group_cell(group, index)
+                line = line_at(index)
+                ix, iy = line // 4, line % 4
                 for iz in range(4):
-                    line, lanes = 4 * ix + iy, pl.ds(128 * iz, 128)
+                    lanes = pl.ds(128 * iz, 128)
                     slope = 3.0 * slo[e, ix, iy, iz]
                     keep(line, 8, lanes, slope)
                     for k in range(3):
                         rows[line, 5 + k, :, lanes] = slope * rows[line, 2 + k, :, lanes]
                 return carry
 
-            lax.fori_loop(0, 4, spread, 0)
+            lax.fori_loop(0, count, spread, 0)
             add_forces(group)
         kick = jnp.where(e == 1, 2.0, 1.0) * (0.5 * time_step)
         for y, z in cells:
@@ -280,7 +318,7 @@
             out_vel[k, y, pl.ds(z, 1)] = vel[2 * y + z][k : k + 1]
 
     def drain(e, carry):
-        for group in range(3):
+        for group in range(5):
             wait(ext, e, pos_send, group)
             wait(slo, e, slo_send, group)
         return carry
@@ -294,7 +332,7 @@
     new_positions, new_velocities = pl.pallas_call(
         kernel,
         out_shape=(shape, shape),
-        in_specs=[vmem, vmem, vmem, pl.BlockSpec(memory_space=pltpu.SMEM)],
+        in_specs=[pl.BlockSpec(memory_space=pltpu.HBM)] * 4,
         out_specs=(vmem, vmem),
         scratch_shapes=[
             pltpu.VMEM((4, 3, 4, 4, 4, 128), f32),
@@ -308,11 +346,14 @@
             pltpu.VMEM((4, 4, 128), f32),
             pltpu.VMEM((4, 4, 128), f32),
         ]
-        + [pltpu.SemaphoreType.DMA((3, 3))] * 4,
+        + [pltpu.VMEM((3, 2, 2, 128), f32)] * 2
+        + [pltpu.VMEM((2, 2, 128), jnp.int32), pltpu.VMEM((2, 2), jnp.int32)]
+        + [pltpu.SemaphoreType.DMA((3, 5))] * 4
+        + [pltpu.SemaphoreType.DMA((4,))],
         compiler_params=pltpu.CompilerParams(
             collective_id=0, has_side_effects=True, vmem_limit_bytes=32 * 1024 * 1024
         ),
-    )(positions[:, 0], velocities[:, 0], species[0], counts[0])
+    )(*(pltpu.with_memory_space_constraint(a, pltpu.HBM) for a in (positions[:, 0], velocities[:, 0], species[0], counts[0])))
     return new_positions[:, None], new_velocities[:, None]
 
 

time: 73 us -> 66.7 us (0.914)
  Pallas kernels: 68.9 us -> 64.7 us
  local copies, waits for them, and re-layouts: 3.24 us -> 1.19 us
    pallas_call x1, Pallas kernels: 68.9 us -> 64.7 us  [on_device(): pl.pallas_call(kernel, out_shape=(shape, shape), in_specs=[pl.BlockSpec(m...]
    unnamed x10 -> x2, local copies, waits for them, and re-layouts: 3.24 us -> 1.19 us
where the time goes in v2:
time: 66.7 us; the launch traced here: 66.5 us
  Pallas kernels  64.7 us (97%)
  local copies, waits for them, and re-layouts  1.19 us (2%)
    pallas_call x1, Pallas kernels, on_device(): pl.pallas_call(kernel, out_shape=(shape, shape), in_specs=[pl.BlockSpec(m...  64.7 us

profile of v2, /device:TPU:1, one launch (start us, length us, event | category | flops | bytes accessed | tf_op | source)
XLA Modules:
  0.0 66.5 jit_solution(14620486504729048659)
XLA Ops:
  0.6 64.7 %shard_map.59 = (f32[3,2,2,128]{3,2,1,0:T(2,128)S(1)}, f32[3,2,2,128]{3,2,1,0:T(2,128)S(1)}) custom-call(f32[3,2,2,128]{3,2,1,0:T(2,128)} %bitcast.12, f32[3,2,2,128]{3,2,1,0:T(2,128)} %bitcast.13, s32[2,2,128]{2,1,0:T(2,128)} %bitcast.14, s32[2,2]{1,0:T(2,128)} %bitcast.15), custom_call_target="tpu_custom_call" | custom-call | tf_op jit(solution)/shard_map/pallas_call | solution.py:332
  65.3 0.6 copy.10
  65.9 0.6 copy.11

commit v3 on v2

--- a/solution.py
+++ b/solution.py
@@ -24,12 +24,14 @@
 def group_of(d):
     if d[0] == 0:
         return 0 if d[1] == 0 else 1
-    return {0: 2, 1: 3, -1: 4}[d[1]]
+    if d[1] == 0:
+        return 2 if d[2] == 0 else 3
+    return 4 if d[1] == 1 else 5
 
 
 def group_ref(buffer, group):
-    if isinstance(group, int) and group < 3:
-        return (buffer.at[1, 0], buffer.at[1, pl.ds(0, 2)], buffer.at[0])[group]
+    if isinstance(group, int) and group == 0:
+        return buffer.at[1, 0]
     return buffer.at[1, pl.ds(0, 2)]
 
 
@@ -45,7 +47,7 @@
 
 
 def kernel(
-    pos_hbm, vel_hbm, spec_hbm, count_hbm, out_pos, out_vel,
+    pos_hbm, vel_hbm, spec_hbm, count_hbm, out_pos, out_vel, out_push,
     ext, slo, part, rows, lhs, own, near, acc, total, vel,
     pos_ref, vel_ref, spec_ref, count_ref, pos_send, pos_recv, slo_send, slo_recv, load_sem,
 ):
@@ -108,11 +110,11 @@
     def keep(line, k, lanes, value):
         rows[line, k, :, lanes] = jnp.broadcast_to(value, (8, 128))
 
-    def prepare(e, count, line_at):
+    def prepare(e, columns, count, line_at):
         def one(index, carry):
             line = line_at(index)
             ix, iy = line // 4, line % 4
-            for iz in range(4):
+            for iz in columns:
                 lanes = pl.ds(128 * iz, 128)
                 tile = ext[e, ix, iy, iz]
                 place_ = tile + shift_of(ix, iy, iz)
@@ -131,56 +133,54 @@
         lax.fori_loop(0, count, one, 0)
 
     last = lax.rem(place[0] + 1, 2)
-    side_of = {3: 1 - last, 4: last}
+    side_of = {4: 1 - last, 5: last}
 
     fetched = {
         0: (2, lambda k: 5 + k),
         1: (2, lambda k: 4 + 3 * k),
         2: (4, lambda k: 8 * (k // 2) + 1 + k % 2),
-        3: (2, lambda k: 8 * k + 3 * side_of[3]),
         4: (2, lambda k: 8 * k + 3 * side_of[4]),
+        5: (2, lambda k: 8 * k + 3 * side_of[5]),
     }
-
-    def met(group):
-        if group == 0:
-            return [(y, [5, 6]) for y in range(2)]
-        if group == 1:
-            return [(y, [4 + 3 * y]) for y in range(2)]
-        if group == 2:
-            return [(y, [1, 2, 9, 10]) for y in range(2)]
-        y = side_of[group]
-        return [(y, [3 * y, 8 + 3 * y])]
-
-    def strip(c, line, z):
-        t = jnp.dot(lhs[c], part[line, :, pl.ds(128 * z, 384)], preferred_element_type=f32)
-        s = jnp.maximum(t, 0.0)
-        near[c, line] = s
-        return s
 
     def weighted(s, line, z):
         out = None
-        for k in range(3):
+        for k in range(s.shape[1] // 128):
             v = fold(s[:, 128 * k : 128 * k + 128])
             v = v * v * (v * rows[line, 0, :, pl.ds(128 * (z + k), 128)])
             out = v if out is None else out + v
         return out.reshape(128, 128)
 
-    def densities(group):
-        if group == 2:
-
-            def step(k, carry):
-                line = 8 * (k // 2) + 1 + k % 2
-                for y, z in cells:
-                    c = 2 * y + z
-                    acc[c, 0] += weighted(strip(c, line, z), line, z)
-                return carry
-
-            lax.fori_loop(0, 4, step, 0)
-        else:
-            for y, lines in met(group):
-                for z in range(2):
-                    c = 2 * y + z
-                    acc[c, 0] += sum(weighted(strip(c, line, z), line, z) for line in lines)
+    def smooth(first, count, line, lanes):
+        t = jnp.dot(lhs[pl.ds(first, count)], part[line, :, lanes], preferred_element_type=f32)
+        return jnp.maximum(t, 0.0)
+
+    def strips(y, lines):
+        for z in range(2):
+            total_ = 0.0
+            for line in lines:
+                s = smooth(pl.multiple_of(256 * z + 128 * y, 128), 128, line, pl.ds(128 * z, 384))
+                near[2 * y + z, line] = s
+                total_ = total_ + weighted(s, line, z)
+            acc[2 * y + z, 0] += total_
+
+    def core(line):
+        s = smooth(0, 512, line, pl.ds(128, 256))
+        for y, z in cells:
+            mine = s[256 * z + 128 * y : 256 * z + 128 * y + 128]
+            near[2 * y + z, line, :, pl.ds(128 - 128 * z, 256)] = mine
+            acc[2 * y + z, 0] += weighted(mine, line, 1)
+
+    def rim(lines):
+        for z in range(2):
+            found = [smooth(256 * z, 256, line, pl.ds(384 * z, 128)) for line in lines]
+            for y in range(2):
+                extra = 0.0
+                for line, s in zip(lines, found):
+                    mine = s[128 * y : 128 * y + 128]
+                    near[2 * y + z, line, :, pl.ds(256 * z, 128)] = mine
+                    extra = extra + weighted(mine, line, 3 * z)
+                acc[2 * y + z, 0] += extra
 
     def sweep(count, body):
         def one(index, carry):
@@ -231,7 +231,7 @@
             body(c, {0: [5, 6], 1: [4 + 3 * y], 2: [1, 2, 9, 10]}[group], z)
             return carry
 
-        if group < 3:
+        if group < 4:
             lax.fori_loop(0, 4, one, 0)
         else:
             y = side_of[group]
@@ -245,7 +245,7 @@
         return jnp.transpose(jnp.broadcast_to(value, (128, 128)))
 
     def arrival(group):
-        return group if group < 3 else 3 + side_of[group]
+        return group if group < 4 else 4 + side_of[group]
 
     def evaluate(e, carry):
         send(ext, e, pos_send, pos_recv)
@@ -261,13 +261,31 @@
                 [end(h, -1.0), end(h, -1.0), end(m, 0.0), end(m, 0.0), end(h, -1.0), end(l, 0.0), ends, jnp.zeros_like(h)],
                 axis=0,
             )
-            lhs[c] = jnp.transpose(side).astype(bf16)
+            lhs[pl.ds(256 * z + 128 * y, 128)] = jnp.transpose(side).astype(bf16)
             acc[c, 0] = jnp.zeros((128, 128), f32)
             own[c, 1] = across_rows(strength_of(ext[e, 1, 1 + y, 1 + z][3:4]))
-        for group in range(5):
+        prepare(e, (1, 2), *fetched[0])
+        core(5)
+        core(6)
+        wait(ext, e, pos_recv, 0)
+        prepare(e, (0, 3), *fetched[0])
+        rim([5, 6])
+        wait(ext, e, pos_recv, 2)
+        prepare(e, (1, 2), *fetched[2])
+        for line in (1, 2, 9, 10):
+            core(line)
+        wait(ext, e, pos_recv, 3)
+        prepare(e, (0, 3), *fetched[2])
+        rim([1, 2, 9, 10])
+        wait(ext, e, pos_recv, 1)
+        prepare(e, range(4), *fetched[1])
+        for y in range(2):
+            strips(y, [4 + 3 * y])
+        for group in (4, 5):
             wait(ext, e, pos_recv, arrival(group))
-            prepare(e, *fetched[group])
-            densities(group)
+            prepare(e, range(4), *fetched[group])
+            y = side_of[group]
+            strips(y, [3 * y, 8 + 3 * y])
         for y, z in cells:
             c = 2 * y + z
             amplitude = ext[e, 1, 1 + y, 1 + z][3:4]
@@ -281,8 +299,10 @@
             total[c] = lane_sums(c)
             for k in range(4):
                 acc[c, k] = jnp.zeros((128, 128), f32)
-        for group in range(5):
+        for group in (0, 1, 2, 4, 5):
             wait(slo, e, slo_recv, arrival(group))
+            if group == 2:
+                wait(slo, e, slo_recv, 3)
             count, line_at = fetched[group]
 
             def spread(index, carry):
@@ -306,7 +326,11 @@
             r = total[c] + tile[3:4] * lane_sums(c)
             force = -2.0 * (r - place_ * r[3:4])
             v = vel[c]
-            v = jnp.where(row4 < 3, v + kick * v[3:4] * force, v)
+            push = kick * v[3:4] * force
+            for k in range(3):
+                out_vel[k, y, pl.ds(z, 1)] = v[k : k + 1]
+                out_push[k, y, pl.ds(z, 1)] = push[k : k + 1]
+            v = jnp.where(row4 < 3, v + push, v)
             vel[c] = v
             ext[e + 1, 1, 1 + y, 1 + z] = jnp.where(row4 < 3, tile + time_step * v, tile)
         return carry
@@ -314,11 +338,10 @@
     lax.fori_loop(0, 3, evaluate, 0)
     for y, z in cells:
         for k in range(3):
-            out_pos[k, y, pl.ds(z, 1)] = ext[2, 1, 1 + y, 1 + z][k : k + 1]
-            out_vel[k, y, pl.ds(z, 1)] = vel[2 * y + z][k : k + 1]
+            out_pos[k, y, pl.ds(z, 1)] = ext[1, 1, 1 + y, 1 + z][k : k + 1]
 
     def drain(e, carry):
-        for group in range(5):
+        for group in range(6):
             wait(ext, e, pos_send, group)
             wait(slo, e, slo_send, group)
         return carry
@@ -329,17 +352,17 @@
 def on_device(positions, velocities, species, counts):
     vmem = pl.BlockSpec(memory_space=pltpu.VMEM)
     shape = jax.ShapeDtypeStruct((3, 2, 2, 128), f32)
-    new_positions, new_velocities = pl.pallas_call(
+    before, velocity, push = pl.pallas_call(
         kernel,
-        out_shape=(shape, shape),
+        out_shape=(shape, shape, shape),
         in_specs=[pl.BlockSpec(memory_space=pltpu.HBM)] * 4,
-        out_specs=(vmem, vmem),
+        out_specs=(vmem, vmem, vmem),
         scratch_shapes=[
             pltpu.VMEM((4, 3, 4, 4, 4, 128), f32),
             pltpu.VMEM((3, 3, 4, 4, 1, 128), f32),
             pltpu.VMEM((12, 32, 512), bf16),
             pltpu.VMEM((12, 9, 8, 512), f32),
-            pltpu.VMEM((4, 128, 32), bf16),
+            pltpu.VMEM((512, 32), bf16),
             pltpu.VMEM((4, 2, 128, 128), f32),
             pltpu.VMEM((4, 12, 128, 384), f32),
             pltpu.VMEM((4, 4, 128, 128), f32),
@@ -348,13 +371,13 @@
         ]
         + [pltpu.VMEM((3, 2, 2, 128), f32)] * 2
         + [pltpu.VMEM((2, 2, 128), jnp.int32), pltpu.VMEM((2, 2), jnp.int32)]
-        + [pltpu.SemaphoreType.DMA((3, 5))] * 4
+        + [pltpu.SemaphoreType.DMA((3, 6))] * 4
         + [pltpu.SemaphoreType.DMA((4,))],
         compiler_params=pltpu.CompilerParams(
             collective_id=0, has_side_effects=True, vmem_limit_bytes=32 * 1024 * 1024
         ),
     )(*(pltpu.with_memory_space_constraint(a, pltpu.HBM) for a in (positions[:, 0], velocities[:, 0], species[0], counts[0])))
-    return new_positions[:, None], new_velocities[:, None]
+    return (before + time_step * velocity)[:, None], (velocity + push)[:, None]
 
 
 def solution(mesh):

time: 66.7 us -> 64.5 us (0.967)
  Pallas kernels: 64.7 us -> 63.1 us
  local copies, waits for them, and re-layouts: 1.19 us -> 0 us
    pallas_call x1, Pallas kernels: 64.7 us -> 63.1 us  [on_device(): pl.pallas_call(kernel, out_shape=(shape, shape, shape), in_specs=[pl.Bloc...]
    unnamed x2 -> x0, local copies, waits for them, and re-layouts: 1.19 us -> none
where the time goes in v3:
time: 64.5 us; the launch traced here: 64.3 us
  Pallas kernels  63.1 us (98%)
    pallas_call x1, Pallas kernels, on_device(): pl.pallas_call(kernel, out_shape=(shape, shape, shape), in_specs=[pl.Bloc...  63.1 us

profile of v3, /device:TPU:1, one launch (start us, length us, event | category | flops | bytes accessed | tf_op | source)
XLA Modules:
  0.0 64.3 jit_solution(17905181126766367447)
XLA Ops:
  0.6 63.1 %shard_map.59 = (f32[3,2,2,128]{3,2,1,0:T(2,128)S(1)}, f32[3,2,2,128]{3,2,1,0:T(2,128)S(1)}, f32[3,2,2,128]{3,2,1,0:T(2,128)S(1)}) custom-call(f32[3,2,2,128]{3,2,1,0:T(2,128)} %bitcast.12, f32[3,2,2,128]{3,2,1,0:T(2,128)} %bitcast.13, s32[2,2,128]{2,1,0:T(2,128)} %bitcast.14, s32[2,2]{1,0:T(2,128)} %bitcast.15), custom_call_target="tpu_custom_call" | custom-call | tf_op jit(solution)/shard_map/pallas_call | solution.py:355
  63.7 0.6 add_bitcast_fusion

commit v4 on v3

--- a/solution.py
+++ b/solution.py
@@ -86,18 +86,30 @@
 
     pl.semaphore_wait(barrier, len(DIRECTIONS))
 
-    def send(buffer, e, send_sem, recv_sem):
+    last = lax.rem(place[0] + 1, 2)
+    side_of = {4: 1 - last, 5: last}
+
+    def copy_out(buffer, e, send_sem, recv_sem, group, source, target, d):
+        (sz, nz), tz = SOURCE[d[2]], TARGET[d[2]]
+        pltpu.make_async_remote_copy(
+            src_ref=buffer.at[e, 1, source, pl.ds(sz, nz)],
+            dst_ref=buffer.at[e, 1 - d[0], target, pl.ds(tz, nz)],
+            send_sem=send_sem.at[e, group],
+            recv_sem=recv_sem.at[e, group],
+            device_id=device(d),
+            device_id_type=MESH,
+        ).start()
+
+    def send_row(y, *where):
+        for dx in (-1, 1, 0):
+            for dz in (-1, 1, 0):
+                group = 5 - y if dx else 1
+                copy_out(*where, group, pl.ds(1 + y, 1), pl.ds(3 * (1 - y), 1), (dx, 2 * y - 1, dz))
+
+    def send_level(*where):
         for d in DIRECTIONS:
-            dx, dy, dz = d
-            (sy, ny), (sz, nz) = SOURCE[dy], SOURCE[dz]
-            pltpu.make_async_remote_copy(
-                src_ref=buffer.at[e, 1, pl.ds(sy, ny), pl.ds(sz, nz)],
-                dst_ref=buffer.at[e, 1 - dx, pl.ds(TARGET[dy], ny), pl.ds(TARGET[dz], nz)],
-                send_sem=send_sem.at[e, group_of(d)],
-                recv_sem=recv_sem.at[e, group_of(d)],
-                device_id=device(d),
-                device_id_type=MESH,
-            ).start()
+            if d[1] == 0:
+                copy_out(*where, group_of(d), pl.ds(1, 2), pl.ds(1, 2), d)
 
     def wait(buffer, e, sem, group):
         ref = group_ref(buffer.at[e], group)
@@ -132,9 +144,6 @@
 
         lax.fori_loop(0, count, one, 0)
 
-    last = lax.rem(place[0] + 1, 2)
-    side_of = {4: 1 - last, 5: last}
-
     fetched = {
         0: (2, lambda k: 5 + k),
         1: (2, lambda k: 4 + 3 * k),
@@ -247,8 +256,23 @@
     def arrival(group):
         return group if group < 4 else 4 + side_of[group]
 
+    def advance(e, y, z):
+        kick = jnp.where(e == 1, 2.0, 1.0) * (0.5 * time_step)
+        c = 2 * y + z
+        tile = ext[e, 1, 1 + y, 1 + z]
+        place_ = tile + shift_of(1, 1 + y, 1 + z)
+        r = total[c] + tile[3:4] * lane_sums(c)
+        force = -2.0 * (r - place_ * r[3:4])
+        v = vel[c]
+        push = kick * v[3:4] * force
+        for k in range(3):
+            out_vel[k, y, pl.ds(z, 1)] = v[k : k + 1]
+            out_push[k, y, pl.ds(z, 1)] = push[k : k + 1]
+        v = jnp.where(row4 < 3, v + push, v)
+        vel[c] = v
+        ext[e + 1, 1, 1 + y, 1 + z] = jnp.where(row4 < 3, tile + time_step * v, tile)
+
     def evaluate(e, carry):
-        send(ext, e, pos_send, pos_recv)
         for y, z in cells:
             c = 2 * y + z
             place_ = ext[e, 1, 1 + y, 1 + z] + shift_of(1, 1 + y, 1 + z)
@@ -286,12 +310,12 @@
             prepare(e, range(4), *fetched[group])
             y = side_of[group]
             strips(y, [3 * y, 8 + 3 * y])
-        for y, z in cells:
-            c = 2 * y + z
-            amplitude = ext[e, 1, 1 + y, 1 + z][3:4]
-            level = jnp.sum(jnp.transpose(acc[c, 0]), axis=0, keepdims=True) - amplitude + 1.0
-            slo[e, 1, 1 + y, 1 + z] = jnp.where(amplitude > 0.0, -0.5, 0.0) / jnp.sqrt(level)
-        send(slo, e, slo_send, slo_recv)
+            for z in range(2):
+                amplitude = ext[e, 1, 1 + y, 1 + z][3:4]
+                level = jnp.sum(jnp.transpose(acc[2 * y + z, 0]), axis=0, keepdims=True) - amplitude + 1.0
+                slo[e, 1, 1 + y, 1 + z] = jnp.where(amplitude > 0.0, -0.5, 0.0) / jnp.sqrt(level)
+            send_row(y, slo, e, slo_send, slo_recv)
+        send_level(slo, e, slo_send, slo_recv)
         for y, z in cells:
             own[2 * y + z, 0] = across_rows(3.0 * slo[e, 1, 1 + y, 1 + z])
         first_forces()
@@ -318,23 +342,26 @@
 
             lax.fori_loop(0, count, spread, 0)
             add_forces(group)
-        kick = jnp.where(e == 1, 2.0, 1.0) * (0.5 * time_step)
-        for y, z in cells:
-            c = 2 * y + z
-            tile = ext[e, 1, 1 + y, 1 + z]
-            place_ = tile + shift_of(1, 1 + y, 1 + z)
-            r = total[c] + tile[3:4] * lane_sums(c)
-            force = -2.0 * (r - place_ * r[3:4])
-            v = vel[c]
-            push = kick * v[3:4] * force
-            for k in range(3):
-                out_vel[k, y, pl.ds(z, 1)] = v[k : k + 1]
-                out_push[k, y, pl.ds(z, 1)] = push[k : k + 1]
-            v = jnp.where(row4 < 3, v + push, v)
-            vel[c] = v
-            ext[e + 1, 1, 1 + y, 1 + z] = jnp.where(row4 < 3, tile + time_step * v, tile)
+
+            if group < 4:
+                continue
+            y = side_of[group]
+            for z in range(2):
+                advance(e, y, z)
+
+            @pl.when(e < 2)
+            def _():
+                send_row(y, ext, e + 1, pos_send, pos_recv)
+
+        @pl.when(e < 2)
+        def _():
+            send_level(ext, e + 1, pos_send, pos_recv)
+
         return carry
 
+    send_row(side_of[5], ext, 0, pos_send, pos_recv)
+    send_level(ext, 0, pos_send, pos_recv)
+    send_row(side_of[4], ext, 0, pos_send, pos_recv)
     lax.fori_loop(0, 3, evaluate, 0)
     for y, z in cells:
         for k in range(3):

time: 64.5 us -> 63.8 us (0.989)
  Pallas kernels: 63.1 us -> 62.4 us
    pallas_call x1, Pallas kernels: 63.1 us -> 62.4 us  [on_device(): pl.pallas_call(kernel, out_shape=(shape, shape, shape), in_specs=[pl.Bloc...]
where the time goes in v4:
time: 63.8 us; the launch traced here: 63.6 us
  Pallas kernels  62.4 us (98%)
  between operations  0.64 us (1%)
    pallas_call x1, Pallas kernels, on_device(): pl.pallas_call(kernel, out_shape=(shape, shape, shape), in_specs=[pl.Bloc...  62.4 us

profile of v4, /device:TPU:1, one launch (start us, length us, event | category | flops | bytes accessed | tf_op | source)
XLA Modules:
  0.0 63.6 jit_solution(16015164653387326905)
XLA Ops:
  0.6 62.4 %shard_map.59 = (f32[3,2,2,128]{3,2,1,0:T(2,128)S(1)}, f32[3,2,2,128]{3,2,1,0:T(2,128)S(1)}, f32[3,2,2,128]{3,2,1,0:T(2,128)S(1)}) custom-call(f32[3,2,2,128]{3,2,1,0:T(2,128)} %bitcast.12, f32[3,2,2,128]{3,2,1,0:T(2,128)} %bitcast.13, s32[2,2,128]{2,1,0:T(2,128)} %bitcast.14, s32[2,2]{1,0:T(2,128)} %bitcast.15), custom_call_target="tpu_custom_call" | custom-call | tf_op jit(solution)/shard_map/pallas_call | solution.py:382
  63.0 0.6 add_bitcast_fusion

commit v5 on v4

--- a/solution.py
+++ b/solution.py
@@ -208,18 +208,33 @@
     def fold(value):
         return value.reshape(-1, 8, 128)
 
+    def outer(z):
+        return pl.ds(pl.multiple_of(256 * z, 128), 128), pl.ds(pl.multiple_of(384 * z, 128), 128)
+
     def first_forces():
         def body(c, y, z, chunk):
-            slope, strength = fold(own[c, 0, chunk]), fold(own[c, 1, chunk])
+            slope, strength, amplitude = (fold(own[c, k, chunk]) for k in range(3))
             sums = [jnp.zeros(slope.shape, f32) for _ in range(4)]
-            for line, at, lanes in tiles([4 * ix + y + k for ix in range(3) for k in range(3)], z):
+
+            def add(line, at, lanes, known):
                 s = fold(near[c, line, chunk, at])
                 square = s * s
-                near[c, line, chunk, at] = square.reshape(-1, 128)
-                w = square * (slope * rows[line, 0, :, lanes]) + s * (strength * rows[line, 1, :, lanes])
+                pull = slope * rows[line, 0, :, lanes]
+                if known:
+                    pull = pull + amplitude * rows[line, 8, :, lanes]
+                else:
+                    near[c, line, chunk, at] = square.reshape(-1, 128)
+                w = square * pull + s * (strength * rows[line, 1, :, lanes])
                 sums[3] = sums[3] + w
                 for k in range(3):
                     sums[k] = sums[k] + w * rows[line, 2 + k, :, lanes]
+
+            for line in (5, 6):
+                for column in (1, 2):
+                    add(line, pl.ds(pl.multiple_of(128 * (column - z), 128), 128), pl.ds(128 * column, 128), True)
+                add(line, *outer(z), False)
+            for tile in tiles([4 + 3 * y] + [4 * ix + y + k for ix in (0, 2) for k in range(3)], z):
+                add(*tile, False)
             for k in range(4):
                 acc[c, k, chunk] = sums[k].reshape(-1, 128)
 
@@ -228,7 +243,7 @@
     def add_forces(group):
         def body(c, lines, z):
             sums = [fold(acc[c, k]) for k in range(4)]
-            for line, at, lanes in tiles(lines, z):
+            for line, at, lanes in [(line, *outer(z)) for line in lines] if group == 0 else tiles(lines, z):
                 square = fold(near[c, line, :, at])
                 for k in range(4):
                     sums[k] = sums[k] + square * rows[line, 5 + k, :, lanes]
@@ -288,6 +303,7 @@
             lhs[pl.ds(256 * z + 128 * y, 128)] = jnp.transpose(side).astype(bf16)
             acc[c, 0] = jnp.zeros((128, 128), f32)
             own[c, 1] = across_rows(strength_of(ext[e, 1, 1 + y, 1 + z][3:4]))
+            own[c, 2] = across_rows(ext[e, 1, 1 + y, 1 + z][3:4])
         prepare(e, (1, 2), *fetched[0])
         core(5)
         core(6)
@@ -318,6 +334,7 @@
         send_level(slo, e, slo_send, slo_recv)
         for y, z in cells:
             own[2 * y + z, 0] = across_rows(3.0 * slo[e, 1, 1 + y, 1 + z])
+            keep(5 + y, 8, pl.ds(128 + 128 * z, 128), 3.0 * slo[e, 1, 1 + y, 1 + z])
         first_forces()
         for c in range(4):
             total[c] = lane_sums(c)
@@ -390,7 +407,7 @@
             pltpu.VMEM((12, 32, 512), bf16),
             pltpu.VMEM((12, 9, 8, 512), f32),
             pltpu.VMEM((512, 32), bf16),
-            pltpu.VMEM((4, 2, 128, 128), f32),
+            pltpu.VMEM((4, 3, 128, 128), f32),
             pltpu.VMEM((4, 12, 128, 384), f32),
             pltpu.VMEM((4, 4, 128, 128), f32),
             pltpu.VMEM((4, 4, 128), f32),

time: 63.8 us -> 63.8 us (level)
  no operation moved by 1% of the time
where the time goes in v5:
time: 63.8 us; the launch traced here: 63.6 us
  Pallas kernels  62.4 us (98%)
  between operations  0.64 us (1%)
    pallas_call x1, Pallas kernels, on_device(): pl.pallas_call(kernel, out_shape=(shape, shape, shape), in_specs=[pl.Bloc...  62.4 us

profile of v5, /device:TPU:1, one launch (start us, length us, event | category | flops | bytes accessed | tf_op | source)
XLA Modules:
  0.0 63.6 jit_solution(5989949846784643135)
XLA Ops:
  0.6 62.4 %shard_map.59 = (f32[3,2,2,128]{3,2,1,0:T(2,128)S(1)}, f32[3,2,2,128]{3,2,1,0:T(2,128)S(1)}, f32[3,2,2,128]{3,2,1,0:T(2,128)S(1)}) custom-call(f32[3,2,2,128]{3,2,1,0:T(2,128)} %bitcast.12, f32[3,2,2,128]{3,2,1,0:T(2,128)} %bitcast.13, s32[2,2,128]{2,1,0:T(2,128)} %bitcast.14, s32[2,2]{1,0:T(2,128)} %bitcast.15), custom_call_target="tpu_custom_call" | custom-call | tf_op jit(solution)/shard_map/pallas_call | solution.py:399
  63.0 0.6 add_bitcast_fusion
